TPU v7x, 32 devices: a whole 2x2x4 slice. The times are simulated.
32 devices in a mesh: fsdp: 8 (over z, x), rep: 4 (over y, core).
Axes of the slice: x: 2, y: 2, z: 4, core: 2. Of those that a mesh axis runs over, the one named last changes fastest.
Arguments:
- tokens: bfloat16 [16384, 768], P(('fsdp', 'rep')), may hold values from -6 to 6
- bucket_item_counts: int32 [32, 4], P(('fsdp', 'rep')), may hold values from 0 to 8, as said below
- slot_item_lengths: int32 [32, 8], P(('fsdp', 'rep')), may hold values from 1 to 512, as said below
- frozen: bfloat16 [7099392], P(('fsdp', 'rep')), as said below
- query_lowrank_matrix: float32 [8, 768], replicated, may hold values from -1.2 to 1.2
- value_lowrank_matrix: float32 [8, 768], replicated, may hold values from -1.2 to 1.2
- output_gradient: bfloat16 [16384, 768], P(('fsdp', 'rep')), may hold values from -12 to 12
- evaluation_tokens: bfloat16 [65536, 768], P(('fsdp', 'rep')), may hold values from -6 to 6
- evaluation_lengths: int32 [128], P(('fsdp', 'rep')), may hold values from 128 to 512
Outputs:
- layer_training_output: bfloat16 [16384, 768], P(('fsdp', 'rep'))
- token_gradient: float32 [16384, 768], P(('fsdp', 'rep'))
- query_lowrank_gradient: float32 [8, 768], replicated
- value_lowrank_gradient: float32 [8, 768], replicated
- evaluation_output: bfloat16 [65536, 768], P(('fsdp', 'rep'))
Inputs may be any that keep to these rules, and one draw needn't show every extreme that they name: `bucket_item_counts`: each device's counts fill its 512 tokens exactly; items never cross a boundary of 512 rows. `slot_item_lengths`: slot j of a device belongs to its j-th item, whose length lies between half its bucket plus one and its bucket; slots past a device's items hold 1. `frozen`: laid out as the first step says.
All inputs are finite; a program needn't handle non-finite values.
Results may differ from a plain program's by a relative error of at most 0.015.
The roundings to bfloat16 on the way count: a program that leaves them out, or rounds other values in their place, can miss the bound.
Values may be sent and summed in bfloat16 or wider, within the bound.
No kernel may reach another device: no remote copies, remote signals or barrier semaphores. Data moves between devices by JAX's collectives and lax.ppermute only.
A program may use at most 192 MiB of HBM per device.

v0:
```python
from functools import partial

import jax
import jax.numpy as jnp
from jax import lax
from jax.sharding import PartitionSpec as P

MODEL_WIDTH = 768
HEADS = 12
HEAD_DIM = 64
HIDDEN_UNITS = 3072
BUCKET = 512


adapter_scale = 2.0
norm_eps = 1e-05
masked_score = -1e30


def product_single_precision(left, right):
    return jnp.dot(left, right, preferred_element_type=jnp.float32)


def product_backward(left, right):
    return lax.dot_general(
        left, right, (((1,), (1,)), ((), ())), preferred_element_type=jnp.float32
    )


def product_over_rows(left, right):
    return lax.dot_general(
        left, right, (((0,), (0,)), ((), ())), preferred_element_type=jnp.float32
    )


def cast_to_single(value):
    return value.astype(jnp.float32)


def unpack_parameters(
    flattened_parameters, hidden_model_width, feedforward_width, adapter_rank_size
):
    parameter_pieces = [
        ("w_query", (hidden_model_width, hidden_model_width)),
        ("w_key", (hidden_model_width, hidden_model_width)),
        ("w_value", (hidden_model_width, hidden_model_width)),
        ("w_out", (hidden_model_width, hidden_model_width)),
        ("w_up", (hidden_model_width, feedforward_width)),
        ("w_down", (feedforward_width, hidden_model_width)),
        ("b_query", (hidden_model_width,)),
        ("b_value", (hidden_model_width,)),
        ("b_out", (hidden_model_width,)),
        ("b_up", (feedforward_width,)),
        ("b_down", (hidden_model_width,)),
        ("gain_one", (hidden_model_width,)),
        ("shift_one", (hidden_model_width,)),
        ("gain_two", (hidden_model_width,)),
        ("shift_two", (hidden_model_width,)),
        ("a_query", (hidden_model_width, adapter_rank_size)),
        ("a_value", (hidden_model_width, adapter_rank_size)),
    ]
    parameter_set = {}
    offset_at = 0
    for piece_name, piece_shape in parameter_pieces:
        entry_count = 1
        for extent in piece_shape:
            entry_count = entry_count * extent
        parameter_set[piece_name] = flattened_parameters[
            offset_at : offset_at + entry_count
        ].reshape(piece_shape)
        offset_at = offset_at + entry_count
    return parameter_set


def collect_pieces(frozen):
    return lax.all_gather(frozen, ("fsdp", "rep"), axis=0, tiled=True)


def token_layout(counts, lengths, row_total, block_rows):
    position = jnp.arange(row_total, dtype=jnp.int32)
    item_indices = jnp.zeros((row_total,), jnp.int32)
    offset = jnp.zeros((row_total,), jnp.int32)
    region_start = jnp.zeros((), jnp.int32)
    before = jnp.zeros((), jnp.int32)
    for bucket_level in range(4):
        extent = block_rows // 2**bucket_level
        finish = region_start + counts[bucket_level] * extent
        inside = (position >= region_start) & (position < finish)
        relative = position - region_start
        item_indices = jnp.where(inside, before + relative // extent, item_indices)
        offset = jnp.where(inside, relative % extent, offset)
        region_start = finish
        before = before + counts[bucket_level]
    slot_ids = jnp.arange(lengths.shape[0], dtype=jnp.int32)
    length = jnp.sum(
        jnp.where(item_indices[:, None] == slot_ids[None, :], lengths[None, :], 0), axis=1
    )
    return (item_indices, offset < length)


def layer_norm(resid, norm_gain, norm_shift):
    centred = resid - jnp.mean(resid, axis=-1, keepdims=True)
    spread = jnp.mean(centred * centred, axis=-1, keepdims=True)
    return centred * lax.rsqrt(spread + norm_eps) * norm_gain + norm_shift


def exact_gelu(value):
    return jax.nn.gelu(value, approximate=False)


def split_blocks(array_in, block_count):
    return array_in.reshape((block_count, BUCKET) + array_in.shape[1:])


def masked_scores(head_query, head_key, item_indices, valid_key_mask):
    scores = jnp.einsum(
        "qhd,khd->hqk", head_query, head_key, preferred_element_type=jnp.float32
    ) * HEAD_DIM ** (-0.5)
    allowed = (item_indices[:, None] == item_indices[None, :]) & valid_key_mask[None, :]
    return jnp.where(allowed[None], scores, masked_score)


def attend(block_parts):
    query_rows, key_rows, value_rows, item_indices, valid_key_mask = block_parts
    row_count = query_rows.shape[0]
    head_query = query_rows.reshape(row_count, HEADS, HEAD_DIM)
    head_key = key_rows.reshape(row_count, HEADS, HEAD_DIM)
    head_value = value_rows.reshape(row_count, HEADS, HEAD_DIM)
    scores = masked_scores(head_query, head_key, item_indices, valid_key_mask)
    top_score = jnp.max(scores, axis=-1, keepdims=True)
    expo_scores = jnp.exp(scores - top_score)
    denom_sum = jnp.sum(expo_scores, axis=-1, keepdims=True)
    soft_probs = (expo_scores / denom_sum).astype(jnp.bfloat16)
    context = jnp.einsum("hqk,khd->qhd", soft_probs, head_value, preferred_element_type=jnp.float32)
    log_total = (top_score + jnp.log(denom_sum))[..., 0]
    return (context.reshape(row_count, HEADS * HEAD_DIM).astype(jnp.bfloat16), log_total)


def attend_back(block_parts):
    query_rows, key_rows, value_rows, grad_context, log_total, item_indices, valid_key_mask = (
        block_parts
    )
    row_count = query_rows.shape[0]
    head_query = query_rows.reshape(row_count, HEADS, HEAD_DIM)
    head_key = key_rows.reshape(row_count, HEADS, HEAD_DIM)
    head_value = value_rows.reshape(row_count, HEADS, HEAD_DIM)
    grad_heads = grad_context.reshape(row_count, HEADS, HEAD_DIM)
    scores = masked_scores(head_query, head_key, item_indices, valid_key_mask)
    soft_probs = jnp.exp(scores - log_total[..., None])
    value_gradient = jnp.einsum(
        "hqk,qhd->khd",
        soft_probs.astype(jnp.bfloat16),
        grad_heads,
        preferred_element_type=jnp.float32,
    )
    grad_probs = jnp.einsum(
        "qhd,khd->hqk", grad_heads, head_value, preferred_element_type=jnp.float32
    )
    row_dot = jnp.sum(soft_probs * grad_probs, axis=-1, keepdims=True)
    grad_scores = (soft_probs * (grad_probs - row_dot)).astype(jnp.bfloat16)
    query_gradient = jnp.einsum(
        "hqk,khd->qhd", grad_scores, head_key, preferred_element_type=jnp.float32
    ) * HEAD_DIM ** (-0.5)
    grad_key = jnp.einsum(
        "hqk,qhd->khd", grad_scores, head_query, preferred_element_type=jnp.float32
    ) * HEAD_DIM ** (-0.5)
    hidden_model_width = HEADS * HEAD_DIM
    return (
        query_gradient.reshape(row_count, hidden_model_width).astype(jnp.bfloat16),
        grad_key.reshape(row_count, hidden_model_width).astype(jnp.bfloat16),
        value_gradient.reshape(row_count, hidden_model_width).astype(jnp.bfloat16),
    )


def encoder_layer_forward(input_arrays, parameter_set, adapter_pair, item_indices, valid_key_mask):
    query_complete = product_single_precision(
        input_arrays, parameter_set["w_query"]
    ) + cast_to_single(parameter_set["b_query"])
    value_complete = product_single_precision(
        input_arrays, parameter_set["w_value"]
    ) + cast_to_single(parameter_set["b_value"])
    adapt_rows = None
    if adapter_pair is not None:
        query_adapter_out = product_single_precision(input_arrays, parameter_set["a_query"]).astype(
            jnp.bfloat16
        )
        value_adapter_out = product_single_precision(input_arrays, parameter_set["a_value"]).astype(
            jnp.bfloat16
        )
        query_complete = query_complete + adapter_scale * product_single_precision(
            query_adapter_out, adapter_pair[0]
        )
        value_complete = value_complete + adapter_scale * product_single_precision(
            value_adapter_out, adapter_pair[1]
        )
        adapt_rows = (query_adapter_out, value_adapter_out)
    query_complete = query_complete.astype(jnp.bfloat16)
    key_full = product_single_precision(input_arrays, parameter_set["w_key"]).astype(jnp.bfloat16)
    value_complete = value_complete.astype(jnp.bfloat16)
    row_count = input_arrays.shape[0]
    block_count = row_count // BUCKET
    context, log_total = lax.map(
        attend,
        (
            split_blocks(query_complete, block_count),
            split_blocks(key_full, block_count),
            split_blocks(value_complete, block_count),
            split_blocks(item_indices, block_count),
            split_blocks(valid_key_mask, block_count),
        ),
    )
    context = context.reshape(row_count, HEADS * HEAD_DIM)
    resid_one = cast_to_single(input_arrays) + (
        product_single_precision(context, parameter_set["w_out"])
        + cast_to_single(parameter_set["b_out"])
    )
    norm_one = partial(
        layer_norm,
        norm_gain=cast_to_single(parameter_set["gain_one"]),
        norm_shift=cast_to_single(parameter_set["shift_one"]),
    )
    hidden_one, pull_one = jax.vjp(norm_one, resid_one)
    hidden_one = hidden_one.astype(jnp.bfloat16)
    up_rows = product_single_precision(hidden_one, parameter_set["w_up"]) + cast_to_single(
        parameter_set["b_up"]
    )
    gelu_rows, pull_gelu = jax.vjp(exact_gelu, up_rows)
    gelu_rows = gelu_rows.astype(jnp.bfloat16)
    resid_two = cast_to_single(hidden_one) + (
        product_single_precision(gelu_rows, parameter_set["w_down"])
        + cast_to_single(parameter_set["b_down"])
    )
    norm_two = partial(
        layer_norm,
        norm_gain=cast_to_single(parameter_set["gain_two"]),
        norm_shift=cast_to_single(parameter_set["shift_two"]),
    )
    layer_training_output, pull_two = jax.vjp(norm_two, resid_two)
    saved_residuals = (
        query_complete,
        key_full,
        value_complete,
        context,
        log_total,
        adapt_rows,
        pull_one,
        pull_gelu,
        pull_two,
    )
    return (layer_training_output.astype(jnp.bfloat16), saved_residuals)


def local(
    tokens,
    bucket_item_counts,
    slot_item_lengths,
    frozen,
    query_lowrank_matrix,
    value_lowrank_matrix,
    output_gradient,
    evaluation_tokens,
    evaluation_lengths,
):
    adapter_rank_size = query_lowrank_matrix.shape[0]
    parameter_set = unpack_parameters(
        collect_pieces(frozen), MODEL_WIDTH, HIDDEN_UNITS, adapter_rank_size
    )
    row_count = tokens.shape[0]
    item_indices, valid_key_mask = token_layout(
        bucket_item_counts[0], slot_item_lengths[0], row_count, BUCKET
    )
    query_lowrank_term = query_lowrank_matrix.astype(jnp.bfloat16)
    value_lowrank_term = value_lowrank_matrix.astype(jnp.bfloat16)
    layer_training_output, saved_residuals = encoder_layer_forward(
        tokens,
        parameter_set,
        (query_lowrank_term, value_lowrank_term),
        item_indices,
        valid_key_mask,
    )
    merged_weights = dict(parameter_set)
    merged_weights["w_query"] = (
        cast_to_single(parameter_set["w_query"])
        + adapter_scale * product_single_precision(parameter_set["a_query"], query_lowrank_term)
    ).astype(jnp.bfloat16)
    merged_weights["w_value"] = (
        cast_to_single(parameter_set["w_value"])
        + adapter_scale * product_single_precision(parameter_set["a_value"], value_lowrank_term)
    ).astype(jnp.bfloat16)
    eval_count = evaluation_tokens.shape[0]
    positions = jnp.arange(eval_count, dtype=jnp.int32)
    eval_valid = positions % BUCKET < jnp.repeat(evaluation_lengths, BUCKET)
    evaluation_output = encoder_layer_forward(
        evaluation_tokens, merged_weights, None, positions // BUCKET, eval_valid
    )[0]
    backward_parameters = unpack_parameters(
        collect_pieces(frozen), MODEL_WIDTH, HIDDEN_UNITS, adapter_rank_size
    )
    (
        query_complete,
        key_full,
        value_complete,
        context,
        log_total,
        adapt_rows,
        pull_one,
        pull_gelu,
        pull_two,
    ) = saved_residuals
    (grad_two,) = pull_two(cast_to_single(output_gradient))
    grad_down = grad_two.astype(jnp.bfloat16)
    (grad_up,) = pull_gelu(product_backward(grad_down, backward_parameters["w_down"]))
    grad_up = grad_up.astype(jnp.bfloat16)
    grad_hidden = (grad_two + product_backward(grad_up, backward_parameters["w_up"])).astype(
        jnp.bfloat16
    )
    (grad_one,) = pull_one(cast_to_single(grad_hidden))
    grad_context = product_backward(
        grad_one.astype(jnp.bfloat16), backward_parameters["w_out"]
    ).astype(jnp.bfloat16)
    block_count = row_count // BUCKET
    query_gradient, grad_key, value_gradient = lax.map(
        attend_back,
        (
            split_blocks(query_complete, block_count),
            split_blocks(key_full, block_count),
            split_blocks(value_complete, block_count),
            split_blocks(grad_context, block_count),
            log_total,
            split_blocks(item_indices, block_count),
            split_blocks(valid_key_mask, block_count),
        ),
    )
    hidden_model_width = HEADS * HEAD_DIM
    query_gradient = query_gradient.reshape(row_count, hidden_model_width)
    grad_key = grad_key.reshape(row_count, hidden_model_width)
    value_gradient = value_gradient.reshape(row_count, hidden_model_width)
    query_adapter_out, value_adapter_out = adapt_rows
    query_adapter_gradient = (
        adapter_scale * product_backward(query_gradient, query_lowrank_term)
    ).astype(jnp.bfloat16)
    value_adapter_gradient = (
        adapter_scale * product_backward(value_gradient, value_lowrank_term)
    ).astype(jnp.bfloat16)
    lowrank_terms = (
        adapter_scale * product_over_rows(query_adapter_out, query_gradient),
        adapter_scale * product_over_rows(value_adapter_out, value_gradient),
    )
    query_lowrank_gradient, value_lowrank_gradient = lax.psum(
        (lowrank_terms[0], lowrank_terms[1]), ("fsdp", "rep")
    )
    token_gradient = (
        grad_one
        + product_backward(query_gradient, backward_parameters["w_query"])
        + product_backward(grad_key, backward_parameters["w_key"])
        + product_backward(value_gradient, backward_parameters["w_value"])
        + product_backward(query_adapter_gradient, backward_parameters["a_query"])
        + product_backward(value_adapter_gradient, backward_parameters["a_value"])
    )
    return (
        layer_training_output,
        token_gradient,
        query_lowrank_gradient,
        value_lowrank_gradient,
        evaluation_output,
    )


def solution(mesh):
    placed = (
        P(("fsdp", "rep"), None),
        P(("fsdp", "rep"), None),
        P(("fsdp", "rep"), None),
        P(("fsdp", "rep")),
        P(),
        P(),
        P(("fsdp", "rep"), None),
        P(("fsdp", "rep"), None),
        P(("fsdp", "rep")),
    )
    return jax.shard_map(
        local,
        mesh=mesh,
        in_specs=placed,
        out_specs=(
            P(("fsdp", "rep"), None),
            P(("fsdp", "rep"), None),
            P(),
            P(),
            P(("fsdp", "rep"), None),
        ),
        check_vma=False,
    )
```

profile of v0, /device:TPU:0, one launch (start us, length us, event | category | flops | bytes accessed | tf_op | source)
XLA Modules:
  0.0 683.0 jit_solution(15648410029137493754)
XLA Ops:
  7.2 5.2 broadcast.678
  12.5 7.6 %dynamic-update-slice = bf16[7099392]{0:T(1024)(128)(2,1)} dynamic-update-slice(bf16[7099392]{0:T(1024)(128)(2,1)} %broadcast.678, bf16[221856]{0:T(1024)(128)(2,1)S(1)} %copy-done.24, u32[]{:T(128)S(6)} %multiply.77) | dynamic-update-slice | bytes 887428
  25.2 3.0 copy.50
  31.1 241.5 %all-reduce.4.cloned.1.call-done = bf16[7099392]{0:T(1024)(128)(2,1)} async-done(((bf16[7099392]{0:T(1024)(128)(2,1)}), bf16[7099392]{0:T(1024)(128)(2,1)}) %all-reduce.4.cloned.1.call-update) | async-done | bytes 14198800
  273.6 4.3 fusion.153
  277.9 3.3 slice.173
  281.2 6.7 convolution_convert_fusion
  289.7 8.3 %fusion.155 = (bf16[2359296]{0:T(1024)(128)(2,1)}, bf16[2359296]{0:T(1024)(128)(2,1)}) fusion(bf16[7099392]{0:T(1024)(128)(2,1)} %all-reduce.4.cloned.1.call-done), kind=kLoop, calls=%fused_computation.285 | loop fusion | bytes 18874368 | tf_op jit(solution)/shard_map/slice | solution.py:68
  298.0 8.2 %slice.180 = bf16[768,3072]{1,0:T(8,128)(2,1)} reshape(bf16[2359296]{0:T(1024)(128)(2,1)} %get-tuple-element.174) | data formatting | bytes 9437184 | tf_op jit(solution)/shard_map/slice | solution.py:68
  306.2 3.4 slice.175
  309.6 3.3 slice.168
  314.8 3.2 fusion.161
  318.0 3.3 fusion.162
  321.4 9.7 %slice.183 = bf16[3072,768]{1,0:T(8,128)(2,1)} reshape(bf16[2359296]{0:T(1024)(128)(2,1)} %get-tuple-element.175) | data formatting | bytes 9437184 | tf_op jit(solution)/shard_map/slice | solution.py:68
  331.9 6.6 add_convert_fusion.2
  340.3 2.1 fusion.35
  342.5 2.6 fusion.23
  345.0 2.0 copy-done
  347.1 6.6 add_convert_fusion.3
  355.6 7.1 %fusion.47 = bf16[12,64,512]{2,1,0:T(8,128)(2,1)S(1)} fusion(bf16[512,12,64]{0,2,1:T(8,128)(2,1)S(1)} %bitcast.157, f32[12,512]{1,0:T(8,128)S(1)} %fusion.23, f32[12,512]{1,0:T(8,128)S(1)} %get-tuple-element.184, f32[12,512,512]{1,2,0:T(8,128)} %copy-done, pred[512,512]{0,1:T(8,128)(4,1)S(1)} %compare_and_fusion.1), kind=kOutput, calls=%fused_computation.112 | convolution fusion | flops 418775040 | bytes 14467072 | tf_op jit(solution)/shard_map/while/body/eval_jaxpr/hqk,khd->qhd/dot_general | solution.py:134
  364.7 15.5 %fusion.25 = (f32[512,3072]{1,0:T(8,128)S(1)}, f32[512,3072]{1,0:T(8,128)S(1)}) fusion(f32[3072]{0:T(1024)S(1)} %slice_convert_fusion, bf16[768,3072]{1,0:T(8,128)(2,1)S(1)} %bitcast.150, f32[512,768]{1,0:T(8,128)S(1)} %get-tuple-element.187, f32[768]{0:T(1024)S(1)} %get-tuple-element.162, f32[768]{0:T(1024)S(1)} %get-tuple-element.163, ...), kind=kOutput, calls=%fused_computation.49 | convolution fusion | flops 2516975616 | bytes 18896896 | tf_op jit(solution)/shard_map/dot_general | solution.py:21
  380.3 3.0 fusion.158
  387.5 15.8 %multiply_reduce_fusion.3 = (f32[512]{0:T(512)S(1)}, bf16[512,768]{1,0:T(8,128)(2,1)}) fusion(f32[512,768]{1,0:T(8,128)S(1)} %get-tuple-element.187, f32[768]{0:T(1024)S(1)} %get-tuple-element.163, f32[512]{0:T(512)S(1)} %broadcast_multiply_fusion.3, bf16[768,3072]{1,0:T(8,128)(2,1)} %slice.180, f32[512,3072]{1,0:T(8,128)} %copy-done.50, ...), kind=kOutput, calls=%fused_computation.96 | convolution fusion | flops 4864867840 | bytes 26769408 | tf_op jit(solution)/shard_map/dot_general | solution.py:25
  406.3 2.1 convolution_convert_fusion.1
  408.7 6.5 fusion.44
  418.1 10.2 %multiply_reduce_fusion = (f32[12,512]{1,0:T(8,128)S(1)}, f32[12,512,512]{1,2,0:T(8,128)}) fusion(f32[12,512]{1,0:T(8,128)S(1)} %log_add_fusion, f32[12,512,512]{1,2,0:T(8,128)} %copy-done, pred[512,512]{0,1:T(8,128)(4,1)S(1)} %compare_and_fusion.1, bf16[512,12,64]{0,2,1:T(8,128)(2,1)S(1)} %bitcast.156, bf16[512,12,64]{0,2,1:T(8,128)(2,1)S(1)} %bitcast.158), kind=kOutput, calls=%fused_computation.40 | convolution fusion | flops 418375680 | bytes 27049984 | tf_op jit(solution)/shard_map/while/body/eval_jaxpr/qhd,khd->hqk/dot_general | solution.py:156
  428.3 7.2 %multiply_convert_fusion = bf16[12,512,512]{1,2,0:T(8,128)(2,1)S(1)} fusion(f32[12,512,512]{1,2,0:T(8,128)} %get-tuple-element.195, f32[12,512]{1,0:T(8,128)S(1)} %get-tuple-element.194, f32[12,512]{1,0:T(8,128)S(1)} %log_add_fusion, f32[12,512,512]{1,2,0:T(8,128)S(1)} %bitcast.136, pred[512,512]{0,1:T(8,128)(4,1)S(1)} %compare_and_fusion.1), kind=kLoop, calls=%fused_computation.39 | loop fusion | flops 18874368 | bytes 31768576 | tf_op jit(solution)/shard_map/while/body/eval_jaxpr/convert_element_type | solution.py:160
  435.5 3.0 multiply_convert_fusion.3
  440.6 2.0 fusion.163
  444.3 4.0 copy.71
  449.2 3.3 copy_bitcast_fusion
  452.5 73.0 %while.2 = (s32[]{:T(128)}, bf16[4,512,768]{2,1,0:T(8,128)(2,1)}, bf16[4,512,768]{1,2,0:T(8,128)(2,1)}, s32[4,512]{1,0:T(4,128)}, pred[4,512]{1,0:T(4,128)(4,1)S...) while((s32[]{:T(128)}, bf16[4,512,768]{2,1,0:T(8,128)(2,1)}, ...), condition=%wide.region_17.18_spmd, body=%wide.region_14.17_spmd.sunk | while | flops 825098752 | bytes 36757104 | solution.py:202
  456.1 7.6 %fusion.241 = (f32[12,512]{1,0:T(8,128)S(1)}, f32[12,512,512]{1,2,0:T(8,128)}) fusion(pred[512,512]{0,1:T(8,128)(4,1)S(1)} %compare_and_fusion.3, bf16[512,12,64]{0,2,1:T(8,128)(2,1)S(1)} %bitcast.140, bf16[512,12,64]{0,2,1:T(8,128)(2,1)S(1)} %bitcast.139), kind=kOutput, calls=%fused_computation.282.clone.1 | convolution fusion | flops 415236608 | bytes 14442496 | tf_op jit(solution)/shard_map/while/body/eval_jaxpr/sub | solution.py:131
  463.7 5.8 fusion.242
  474.4 7.6 %fusion.241 = (f32[12,512]{1,0:T(8,128)S(1)}, f32[12,512,512]{1,2,0:T(8,128)}) fusion(pred[512,512]{0,1:T(8,128)(4,1)S(1)} %compare_and_fusion.3, bf16[512,12,64]{0,2,1:T(8,128)(2,1)S(1)} %bitcast.140, bf16[512,12,64]{0,2,1:T(8,128)(2,1)S(1)} %bitcast.139), kind=kOutput, calls=%fused_computation.282.clone.1 | convolution fusion | flops 415236608 | bytes 14442496 | tf_op jit(solution)/shard_map/while/body/eval_jaxpr/sub | solution.py:131
  482.0 5.8 fusion.242
  492.7 7.6 %fusion.241 = (f32[12,512]{1,0:T(8,128)S(1)}, f32[12,512,512]{1,2,0:T(8,128)}) fusion(pred[512,512]{0,1:T(8,128)(4,1)S(1)} %compare_and_fusion.3, bf16[512,12,64]{0,2,1:T(8,128)(2,1)S(1)} %bitcast.140, bf16[512,12,64]{0,2,1:T(8,128)(2,1)S(1)} %bitcast.139), kind=kOutput, calls=%fused_computation.282.clone.1 | convolution fusion | flops 415236608 | bytes 14442496 | tf_op jit(solution)/shard_map/while/body/eval_jaxpr/sub | solution.py:131
  500.2 5.8 fusion.242
  510.9 7.6 %fusion.241 = (f32[12,512]{1,0:T(8,128)S(1)}, f32[12,512,512]{1,2,0:T(8,128)}) fusion(pred[512,512]{0,1:T(8,128)(4,1)S(1)} %compare_and_fusion.3, bf16[512,12,64]{0,2,1:T(8,128)(2,1)S(1)} %bitcast.140, bf16[512,12,64]{0,2,1:T(8,128)(2,1)S(1)} %bitcast.139), kind=kOutput, calls=%fused_computation.282.clone.1 | convolution fusion | flops 415236608 | bytes 14442496 | tf_op jit(solution)/shard_map/while/body/eval_jaxpr/sub | solution.py:131
  518.5 5.8 fusion.242
  525.5 6.5 fusion.159
  534.7 66.9 %fusion.37.clone.4 = bf16[2048,3072]{1,0:T(8,128)(2,1)} fusion(f32[3072]{0:T(1024)S(1)} %copy-done.38, bf16[768,3072]{1,0:T(8,128)(2,1)S(1)} %bitcast.152, f32[2048,768]{0,1:T(8,128)S(1)} %get-tuple-element.197, f32[768]{0:T(1024)S(1)} %copy-done.45, f32[768]{0:T(1024)S(1)} %copy-done.36, ...), kind=kOutput, calls=%fused_computation.23.clone.clone.clone.clone.clone.clone.1 | convolution fusion | flops 10086776832 | bytes 23627776 | tf_op jit(solution)/shard_map/dot_general | solution.py:21
  601.7 17.9 %fusion.160 = (f32[2048]{0:T(1024)S(1)}, f32[2048,768]{0,1:T(8,128)}) fusion(f32[768]{0:T(1024)S(1)} %copy-done.43, bf16[3072,768]{1,0:T(8,128)(2,1)} %slice.183, f32[768]{0:T(1024)S(1)} %copy-done.45, f32[768]{0:T(1024)S(1)} %copy-done.36, f32[2048]{0:T(1024)S(1)} %add_rsqrt_fusion.1, f32[2048,768]{0,1:T(8,128)} %copy-done.2, ...), kind=kOutput, calls=%fused_computation.290 | convolution fusion | flops 9677830144 | bytes 29918208 | tf_op jit(solution)/shard_map/dot_general | solution.py:21
  619.6 3.6 multiply_reduce_fusion.1
  625.3 2.8 copy.55
  628.1 2.3 fusion.164
  630.4 40.5 %all-reduce.1 = (f32[8,768]{1,0:T(8,128)}, f32[8,768]{1,0:T(8,128)}) all-reduce(f32[8,768]{1,0:T(8,128)S(1)} %copy-done.29, f32[8,768]{1,0:T(8,128)S(1)} %copy-done.28), channel_id=1, replica_groups=mesh['fsdp'=8,'rep'=4] {'fsdp','rep'}, use_global_device_ids=true, to_apply=%region_12.13 | all-reduce | flops 12288 | bytes 98304 | tf_op jit(solution)/shard_map/psum | solution.py:349
  670.9 5.0 add_add_fusion.4
  (199 shorter events, 53.7 us)
Async XLA Ops:
  7.2 265.4 %all-reduce.4.cloned.1.call-start = ((), (), s32[]{:S(2)}) async-start(), calls=%async_computation | async-start | bytes 28397568
  7.2 5.2 copy-start.24
  20.0 5.1 copy-start.8
  20.1 10.1 %copy-start.48 = (s32[1,8]{1,0:T(1,128)S(1)}, s32[1,8]{1,0:T(1,128)}, u32[]{:S(2)}) copy-start(s32[1,8]{1,0:T(1,128)} %param.13) | copy-start | bytes 100
  20.1 10.1 %copy-start.49 = (s32[4]{0:T(128)S(1)}, s32[4]{0:T(128)}, u32[]{:S(2)}) copy-start(s32[4]{0:T(128)} %param.19) | copy-start | bytes 52
  273.6 58.3 %copy-start.14 = (bf16[768,8]{1,0:T(8,128)(2,1)}, bf16[768,8]{1,0:T(8,128)(2,1)S(1)}, u32[]{:S(2)}) copy-start(bf16[768,8]{1,0:T(8,128)(2,1)S(1)} %slice.171) | copy-start | bytes 36868
  281.2 6.7 copy-start.11
  281.2 6.7 copy-start.18
  289.4 57.7 %copy-start.16 = (bf16[768,8]{1,0:T(8,128)(2,1)}, bf16[768,8]{1,0:T(8,128)(2,1)S(1)}, u32[]{:S(2)}) copy-start(bf16[768,8]{1,0:T(8,128)(2,1)S(1)} %slice.162) | copy-start | bytes 36868
  318.0 13.9 %copy-start.20 = (bf16[768,768]{1,0:T(8,128)(2,1)S(1)}, bf16[768,768]{1,0:T(8,128)(2,1)}, u32[]{:S(2)}) copy-start(bf16[768,768]{1,0:T(8,128)(2,1)} %slice.168) | copy-start | bytes 3538948
  318.0 13.9 %copy-start.25 = (f32[8,768]{1,0:T(8,128)S(1)}, f32[8,768]{1,0:T(8,128)}, u32[]{:S(2)}) copy-start(f32[8,768]{1,0:T(8,128)} %param.15) | copy-start | bytes 73732
  331.8 30.9 %copy-start.46 = (f32[768]{0:T(1024)}, f32[768]{0:T(1024)S(1)}, u32[]{:S(2)}) copy-start(f32[768]{0:T(1024)S(1)} %get-tuple-element.164) | copy-start | bytes 9220
  331.9 48.4 %copy-start.42 = (f32[768]{0:T(1024)}, f32[768]{0:T(1024)S(1)}, u32[]{:S(2)}) copy-start(f32[768]{0:T(1024)S(1)} %get-tuple-element.161) | copy-start | bytes 9220
  331.9 48.4 %copy-start.44 = (f32[768]{0:T(1024)}, f32[768]{0:T(1024)S(1)}, u32[]{:S(2)}) copy-start(f32[768]{0:T(1024)S(1)} %get-tuple-element.162) | copy-start | bytes 9220
  331.9 53.5 %copy-start.33 = (f32[768]{0:T(1024)}, f32[768]{0:T(1024)S(1)}, u32[]{:S(2)}) copy-start(f32[768]{0:T(1024)S(1)} %get-tuple-element.167) | copy-start | bytes 9220
  331.9 55.6 %copy-start.31 = (f32[768]{0:T(1024)}, f32[768]{0:T(1024)S(1)}, u32[]{:S(2)}) copy-start(f32[768]{0:T(1024)S(1)} %get-tuple-element.160) | copy-start | bytes 9220
  331.9 71.4 %copy-start.35 = (f32[768]{0:T(1024)}, f32[768]{0:T(1024)S(1)}, u32[]{:S(2)}) copy-start(f32[768]{0:T(1024)S(1)} %get-tuple-element.163) | copy-start | bytes 9220
  342.4 4.6 copy-start
  342.4 4.6 copy-start.22
  342.4 4.6 copy-start.26
  355.5 7.2 %copy-start.5 = (bf16[512,768]{0,1:T(8,128)(2,1)}, bf16[512,768]{0,1:T(8,128)(2,1)S(1)}, u32[]{:S(2)}) copy-start(bf16[512,768]{0,1:T(8,128)(2,1)S(1)} %fusion.43) | copy-start | bytes 2359300
  355.5 9.2 %slice-start.3 = ((s8[4718592]{0:T(1024)(128)(4,1)}), s8[4194304]{0:T(1024)(128)(4,1)S(1)}, s32[]{:S(2)}) async-start(s8[4718592]{0:T(1024)(128)(4,1)} %bitcast.149), calls=%async_computation.4 | async-start | bytes 8388608
  355.5 7.2 %copy-start.12 = (bf16[512,768]{1,0:T(8,128)(2,1)S(1)}, bf16[512,768]{1,0:T(8,128)(2,1)}, u32[]{:S(2)}) copy-start(bf16[512,768]{1,0:T(8,128)(2,1)} %param.11) | copy-start | bytes 2359300
  355.5 7.2 %copy-start.19 = (bf16[768,768]{1,0:T(8,128)(2,1)S(1)}, bf16[768,768]{1,0:T(8,128)(2,1)}, u32[]{:S(2)}) copy-start(bf16[768,768]{1,0:T(8,128)(2,1)} %slice.175) | copy-start | bytes 3538948
  355.6 9.2 %slice-start.4 = ((s8[4718592]{0:T(1024)(128)(4,1)}), s8[524288]{0:T(1024)(128)(4,1)S(1)}, s32[]{:S(2)}) async-start(s8[4718592]{0:T(1024)(128)(4,1)} %bitcast.149), calls=%async_computation.5 | async-start | bytes 1048576
  362.7 17.6 %slice-start.7 = ((s8[4718592]{0:T(1024)(128)(4,1)}), s8[4194304]{0:T(1024)(128)(4,1)S(1)}, s32[]{:S(2)}) async-start(s8[4718592]{0:T(1024)(128)(4,1)} %bitcast.153), calls=%async_computation.8 | async-start | bytes 8388608
  364.7 22.8 %copy-start.37 = (f32[3072]{0:T(1024)}, f32[3072]{0:T(1024)S(1)}, u32[]{:S(2)}) copy-start(f32[3072]{0:T(1024)S(1)} %slice_convert_fusion) | copy-start | bytes 36868
  364.7 15.6 %slice-start.8 = ((s8[4718592]{0:T(1024)(128)(4,1)}), s8[524288]{0:T(1024)(128)(4,1)S(1)}, s32[]{:S(2)}) async-start(s8[4718592]{0:T(1024)(128)(4,1)} %bitcast.153), calls=%async_computation.9 | async-start | bytes 1048576
  380.3 4.5 copy-start.51
  380.3 4.5 copy-start.13
  408.7 7.4 %copy-start.23 = (bf16[768,768]{1,0:T(8,128)(2,1)S(1)}, bf16[768,768]{1,0:T(8,128)(2,1)}, u32[]{:S(2)}) copy-start(bf16[768,768]{1,0:T(8,128)(2,1)} %slice.159) | copy-start | bytes 3538948
  408.7 9.4 %copy-start.6 = (bf16[512,768]{0,1:T(8,128)(2,1)S(1)}, bf16[512,768]{0,1:T(8,128)(2,1)}, u32[]{:S(2)}) copy-start(bf16[512,768]{0,1:T(8,128)(2,1)} %copy-done.5) | copy-start | bytes 2359300
  416.1 12.2 %slice-start = ((s8[12582912]{0:T(1024)(128)(4,1)}), s8[4194304]{0:T(1024)(128)(4,1)S(1)}, s32[]{:S(2)}) async-start(s8[12582912]{0:T(1024)(128)(4,1)} %bitcast.135), calls=%async_computation.1 | async-start | bytes 8388608
  418.1 10.2 %slice-start.1 = ((s8[12582912]{0:T(1024)(128)(4,1)}), s8[4194304]{0:T(1024)(128)(4,1)S(1)}, s32[]{:S(2)}) async-start(s8[12582912]{0:T(1024)(128)(4,1)} %bitcast.135), calls=%async_computation.2 | async-start | bytes 8388608
  418.1 10.2 %slice-start.2 = ((s8[12582912]{0:T(1024)(128)(4,1)}), s8[4194304]{0:T(1024)(128)(4,1)S(1)}, s32[]{:S(2)}) async-start(s8[12582912]{0:T(1024)(128)(4,1)} %bitcast.135), calls=%async_computation.3 | async-start | bytes 8388608
  444.3 4.9 copy-start.10
  452.5 73.0 %copy-start.47 = (f32[768]{0:T(1024)S(1)}, f32[768]{0:T(1024)}, u32[]{:S(2)}) copy-start(f32[768]{0:T(1024)} %copy-done.46) | copy-start | bytes 9220
  525.5 9.2 %slice-start.5 = ((s8[4718592]{0:T(1024)(128)(4,1)}), s8[4194304]{0:T(1024)(128)(4,1)S(1)}, s32[]{:S(2)}) async-start(s8[4718592]{0:T(1024)(128)(4,1)} %bitcast.151), calls=%async_computation.6 | async-start | bytes 8388608
  525.5 9.2 %slice-start.6 = ((s8[4718592]{0:T(1024)(128)(4,1)}), s8[524288]{0:T(1024)(128)(4,1)S(1)}, s32[]{:S(2)}) async-start(s8[4718592]{0:T(1024)(128)(4,1)} %bitcast.151), calls=%async_computation.7 | async-start | bytes 1048576
  534.7 67.0 %copy-start.43 = (f32[768]{0:T(1024)S(1)}, f32[768]{0:T(1024)}, u32[]{:S(2)}) copy-start(f32[768]{0:T(1024)} %copy-done.42) | copy-start | bytes 9220
  619.6 4.6 copy-start.1
  619.6 4.6 copy-start.32
  619.6 4.6 copy-start.34
  625.2 5.2 copy-start.28
  625.2 5.2 copy-start.29
  625.2 45.6 %copy-start.17 = (bf16[768,8]{1,0:T(8,128)(2,1)S(1)}, bf16[768,8]{1,0:T(8,128)(2,1)}, u32[]{:S(2)}) copy-start(bf16[768,8]{1,0:T(8,128)(2,1)} %copy-done.16) | copy-start | bytes 36868
  625.2 45.6 %copy-start.27 = (f32[8,768]{1,0:T(8,128)S(1)}, f32[8,768]{1,0:T(8,128)}, u32[]{:S(2)}) copy-start(f32[8,768]{1,0:T(8,128)} %param.16) | copy-start | bytes 73732
  625.3 45.6 %copy-start.40 = (f32[512]{0:T(512)S(1)}, f32[512]{0:T(512)}, u32[]{:S(2)}) copy-start(f32[512]{0:T(512)} %copy-done.39) | copy-start | bytes 6148
  (14 other events, 32.0 us)
Sparse Core Ops, SparseCore 0:
  20.2 252.3 all-reduce.3
where the time goes:
time: 694 us; the launch traced here: 683 us
  matrix products  259 us (37%)
  waiting for transfers between devices  241 us (35%)
  local copies, waits for them, and re-layouts  98.5 us (14%)
  blocking collectives  40.5 us (6%)
  other arithmetic  24 us (3%)
  between operations  19.5 us (3%)
    unnamed x2, waiting for transfers between devices  241 us
    dot_general x16, matrix products, product_single_precision(): return jnp.dot(left, right, preferred_element_type=jnp.float32)  142 us
    slice x11, local copies, waits for them, and re-layouts, unpack_parameters(): flattened_parameters[offset_at:offset_at + entry_count].reshape(piece_shape)  43.7 us
    psum x1, blocking collectives, local(): lax.psum((lowrank_terms[0], lowrank_terms[1]), ('fsdp', 'rep'))  40.5 us
    dot_general x7, matrix products, product_backward(): lax.dot_general(left, right, (((1,), (1,)), ((), ())), preferred_element_...  31 us
    sub x4, matrix products, attend(): expo_scores = jnp.exp(scores - top_score)  30.3 us
    dot_general x5, matrix products, attend(): jnp.einsum('hqk,khd->qhd', soft_probs, head_value, preferred_element_type...  30.3 us
    unnamed x126, local copies, waits for them, and re-layouts  28.3 us
  transfers between devices with their start and end apart: 1, of which 1 were waited for; matrix products, arithmetic and copies ran while one was open for 1% of the time, Pallas kernels for 0%

commit v1 on v0

v1 whole, which is shorter than its diff:
```python
import functools

import jax
import jax.numpy as jnp
from jax import lax
from jax.experimental import pallas as pl
from jax.experimental.pallas import tpu as pltpu
from jax.sharding import PartitionSpec as P

WIDTH = 768
HEADS = 12
HEAD_DIM = 64
SLABS = 4
BUCKET = 512
CHUNK = 256
PAIR = 2 * HEAD_DIM
PAIRS = HEADS // 2
WEIGHT_ROWS = WIDTH * (4 + 2 * SLABS)
QKV_ROWS = 3 * WIDTH
VECTOR_ROWS = 12
RANK = 8
FORBIDDEN = -1e30
EPS = 1e-5
VMEM = 60 * 2**20

f32 = jnp.float32
bf16 = jnp.bfloat16

BQ, BV, BO, B1, B2, G1, C1, G2, C2 = 0, 1, 2, 3, 7, 8, 9, 10, 11


def dot(left, right):
    return jnp.dot(left, right, preferred_element_type=f32)


def dot_last(left, right):
    return lax.dot_general(left, right, (((1,), (1,)), ((), ())), preferred_element_type=f32)


def dot_first(left, right):
    return lax.dot_general(left, right, (((0,), (0,)), ((), ())), preferred_element_type=f32)


def row(tail_ref, at):
    return tail_ref[...].astype(f32)[at : at + 1]


def normalise(resid):
    centred = resid - jnp.mean(resid, axis=-1, keepdims=True)
    scale = lax.rsqrt(jnp.mean(centred * centred, axis=-1, keepdims=True) + EPS)
    return centred * scale, scale


def normalise_back(grad, normed, scale):
    return scale * (
        grad
        - jnp.mean(grad, axis=-1, keepdims=True)
        - normed * jnp.mean(grad * normed, axis=-1, keepdims=True)
    )


def half_error_function(value):
    return 0.5 + 0.5 * lax.erf(value * 0.7071067811865476)


def gelu(value):
    return value * half_error_function(value)


def gelu_slope(value):
    density = jnp.exp(value * value * -0.5) * 0.3989422804014327
    return half_error_function(value) + value * density


def low_lanes(rows):
    return lax.broadcasted_iota(jnp.int32, (rows, PAIR), 1) < HEAD_DIM


def head_stack(pair):
    low = low_lanes(pair.shape[0])
    zero = jnp.zeros_like(pair)
    return jnp.concatenate([jnp.where(low, pair, zero), jnp.where(low, zero, pair)], axis=0)


def item_masks(counts_ref, lengths_ref):
    position = lax.broadcasted_iota(jnp.int32, (BUCKET, 128), 0)
    column = lax.broadcasted_iota(jnp.int32, (BUCKET, 128), 1)
    start = jnp.zeros((BUCKET, 128), jnp.int32)
    finish = jnp.zeros((BUCKET, 128), jnp.int32)
    valid = jnp.zeros((BUCKET, 128), jnp.int32)
    base = jnp.int32(0)
    first = jnp.int32(0)
    for level in range(counts_ref.shape[1]):
        extent = BUCKET >> level
        count = counts_ref[0, level]
        inside = (column >= first) & (column < first + count)
        here = base + (column - first) * extent
        start = jnp.where(inside, here, start)
        finish = jnp.where(inside, here + extent, finish)
        base = base + count * extent
        first = first + count
    for slot in range(lengths_ref.shape[1]):
        valid = jnp.where(column == slot, lengths_ref[0, slot], valid)
    member = (position >= start) & (position < finish)
    allowed = member & (position < start + valid)
    return (
        jnp.where(member, 1.0, 0.0).astype(bf16),
        jnp.where(allowed, 0.0, FORBIDDEN).astype(bf16),
    )


def attend(q_s, k_s, v_s, query_mask, key_mask, put):
    rows = q_s.shape[0]
    ones = jnp.ones((rows, 128), bf16)
    masks = jnp.concatenate([query_mask, query_mask], axis=0)
    low = low_lanes(rows)

    def scores_of(pair):
        at = slice(PAIR * pair, PAIR * (pair + 1))
        left = jnp.concatenate([head_stack(q_s[:, at]), masks], axis=1)
        return dot_last(left, jnp.concatenate([k_s[:, at], key_mask], axis=1))

    scores = scores_of(0)
    for pair in range(PAIRS):
        later = scores_of(pair + 1) if pair + 1 < PAIRS else None
        at = slice(PAIR * pair, PAIR * (pair + 1))
        top = jnp.max(scores, axis=-1, keepdims=True)
        weights = jnp.exp(scores - top).astype(bf16)
        mixed = dot(weights, jnp.concatenate([v_s[:, at], ones], axis=1))
        mixed = mixed[:, :PAIR] / mixed[:, PAIR:]
        put(at, jnp.where(low, mixed[:rows], mixed[rows:]).astype(bf16))
        scores = later


def train_attention_kernel(
    counts_ref, lengths_ref, x_ref, tail_ref, a_ref, bq_ref, bv_ref, w_any,
    ctx_ref, q_ref, k_ref, v_ref, w, sems,
):
    copies = [
        pltpu.make_async_copy(w_any.at[pl.ds(WIDTH * i, WIDTH)], w.at[i], sems.at[i]) for i in range(3)
    ]
    for copy in copies:
        copy.start()
    query_mask, key_mask = item_masks(counts_ref, lengths_ref)
    x = x_ref[...]
    aq = dot(x, a_ref[0]).astype(bf16)
    av = dot(x, a_ref[1]).astype(bf16)
    copies[0].wait()
    q = dot(x, w[0]) + row(tail_ref, BQ) + 2.0 * dot(aq, bq_ref[...])
    q_ref[...] = (q.astype(bf16).astype(f32) * HEAD_DIM**-0.5).astype(bf16)
    copies[1].wait()
    k_ref[...] = dot(x, w[1]).astype(bf16)
    copies[2].wait()
    v_ref[...] = (dot(x, w[2]) + row(tail_ref, BV) + 2.0 * dot(av, bv_ref[...])).astype(bf16)

    def put(at, value):
        ctx_ref[:, at] = value

    attend(q_ref, k_ref, v_ref, query_mask, key_mask, put)


def eval_attention_kernel(
    lengths_ref, x_ref, tail_ref, a_ref, bq_ref, bv_ref, w_any,
    ctx_ref, w, q_s, k_s, v_s, sems,
):
    step = pl.program_id(0)

    @pl.when(step == 0)
    def _():
        copies = [
            pltpu.make_async_copy(w_any.at[pl.ds(WIDTH * i, WIDTH)], w.at[i], sems.at[i])
            for i in range(3)
        ]
        for copy in copies:
            copy.start()
        for i, b_ref in ((0, bq_ref), (2, bv_ref)):
            copies[i].wait()
            merged = w[i].astype(f32) + 2.0 * dot(a_ref[i // 2], b_ref[...])
            w[i] = merged.astype(bf16)
        copies[1].wait()

    x = x_ref[...]
    q = dot(x, w[0]) + row(tail_ref, BQ)
    q_s[...] = (q.astype(bf16).astype(f32) * HEAD_DIM**-0.5).astype(bf16)
    k_s[...] = dot(x, w[1]).astype(bf16)
    v_s[...] = (dot(x, w[2]) + row(tail_ref, BV)).astype(bf16)
    position = lax.broadcasted_iota(jnp.int32, (BUCKET, 128), 0)
    column = lax.broadcasted_iota(jnp.int32, (BUCKET, 128), 1)
    length = lengths_ref[step]
    key_mask = jnp.where((column > 0) | (position < length), 0.0, FORBIDDEN).astype(bf16)
    query_mask = jnp.where(column == 0, 1.0, 0.0).astype(bf16)

    def put(at, value):
        ctx_ref[:, at] = value

    attend(q_s, k_s, v_s, query_mask, key_mask, put)


def feed_forward(h1, tail_ref, w1, w2, ready, keep):
    per_slab = WIDTH // CHUNK
    chunks = [(slab, CHUNK * part) for slab in range(SLABS) for part in range(per_slab)]

    def up(chunk):
        slab, at = chunk
        if at == 0:
            ready(slab)
        u = dot(h1, w1[slab, :, at : at + CHUNK]) + row(tail_ref, B1 + slab)[:, at : at + CHUNK]
        keep(slab, at, u)
        return u

    total = None
    u = up(chunks[0])
    for i, (slab, at) in enumerate(chunks):
        later = up(chunks[i + 1]) if i + 1 < len(chunks) else None
        part = dot(gelu(u).astype(bf16), w2[slab, at : at + CHUNK, :])
        total = part if total is None else total + part
        u = later
    return total


def eval_tail_kernel(
    x_ref, ctx_ref, tail_ref, wo_any, w1_any, w2_any, out_ref, wo, w1, w2, sems
):
    first = pl.program_id(0) == 0
    copies = [pltpu.make_async_copy(wo_any, wo, sems.at[0])]
    for slab in range(SLABS):
        copies.append(pltpu.make_async_copy(w1_any.at[slab], w1.at[slab], sems.at[1 + 2 * slab]))
        copies.append(pltpu.make_async_copy(w2_any.at[slab], w2.at[slab], sems.at[2 + 2 * slab]))

    @pl.when(first)
    def _():
        for copy in copies:
            copy.start()
        for copy in copies:
            copy.wait()

    resid = x_ref[...].astype(f32) + (dot(ctx_ref[...], wo[...]) + row(tail_ref, BO))
    normed, _ = normalise(resid)
    h1 = (normed * row(tail_ref, G1) + row(tail_ref, C1)).astype(bf16)
    down = feed_forward(h1, tail_ref, w1, w2, lambda slab: None, lambda slab, at, u: None)
    normed, _ = normalise(h1.astype(f32) + (down + row(tail_ref, B2)))
    out_ref[...] = (normed * row(tail_ref, G2) + row(tail_ref, C2)).astype(bf16)


def attention_back(q_ref, k_ref, v_ref, dctx, masks, dq_s, dk_s, dv_s):
    query_mask, key_mask = masks
    rows = q_ref.shape[0]
    masks = jnp.concatenate([query_mask, query_mask], axis=0)
    for pair in range(PAIRS):
        at = slice(PAIR * pair, PAIR * (pair + 1))
        q2, k, v, d2 = head_stack(q_ref[:, at]), k_ref[:, at], v_ref[:, at], head_stack(dctx[:, at])
        scores = dot_last(
            jnp.concatenate([k, key_mask], axis=1), jnp.concatenate([q2, masks], axis=1)
        )
        top = jnp.max(scores, axis=0, keepdims=True)
        probs = jnp.exp(scores - top)
        probs = probs * (1.0 / jnp.sum(probs, axis=0, keepdims=True))
        grad_probs = dot_last(v, d2)
        dv_s[:, at] = dot(probs.astype(bf16), d2).astype(bf16)
        weighted = probs * grad_probs
        inner = jnp.sum(weighted, axis=0, keepdims=True)
        grad_scores = (probs * (grad_probs - inner)).astype(bf16)
        dk_s[:, at] = dot(grad_scores, q2).astype(bf16)
        crossed = dot_first(k, grad_scores)
        dq = jnp.concatenate([crossed[:HEAD_DIM, :rows], crossed[HEAD_DIM:, rows:]], axis=0)
        dq_s[:, at] = (dq.T * HEAD_DIM**-0.5).astype(bf16)


def train_kernel(
    counts_ref, lengths_ref, x_ref, q_ref, k_ref, v_ref, ctx_ref, grad_ref, tail_ref, a_ref, bq_ref, bv_ref,
    w_any, wo_any, w1_any, w2_any,
    out_ref, token_ref, gq_ref, gv_ref,
    w, wo, w1, w2, u_s, dq_s, dk_s, dv_s, sems,
):
    copies = [pltpu.make_async_copy(wo_any, wo, sems.at[0])]
    for slab in range(SLABS):
        copies.append(pltpu.make_async_copy(w1_any.at[slab], w1.at[slab], sems.at[1 + 2 * slab]))
        copies.append(pltpu.make_async_copy(w2_any.at[slab], w2.at[slab], sems.at[2 + 2 * slab]))
    qkv = pltpu.make_async_copy(w_any.at[pl.ds(0, QKV_ROWS)], w, sems.at[1 + 2 * SLABS])
    for copy in [*copies, qkv]:
        copy.start()

    x = x_ref[...]
    copies[0].wait()
    resid = x.astype(f32) + (dot(ctx_ref[...], wo[...]) + row(tail_ref, BO))
    normed_one, scale_one = normalise(resid)
    h1 = (normed_one * row(tail_ref, G1) + row(tail_ref, C1)).astype(bf16)

    def ready(slab):
        copies[1 + 2 * slab].wait()
        copies[2 + 2 * slab].wait()

    def keep(slab, at, u):
        u_s[slab, :, at : at + CHUNK] = u

    down = feed_forward(h1, tail_ref, w1, w2, ready, keep)
    normed_two, scale_two = normalise(h1.astype(f32) + (down + row(tail_ref, B2)))
    out_ref[...] = (normed_two * row(tail_ref, G2) + row(tail_ref, C2)).astype(bf16)

    grad_two = normalise_back(grad_ref[...].astype(f32) * row(tail_ref, G2), normed_two, scale_two)
    df = grad_two.astype(bf16)
    total = None
    for slab in range(SLABS):
        for at in range(0, WIDTH, CHUNK):
            grad_gelu = dot_last(df, w2[slab, at : at + CHUNK, :])
            du = (grad_gelu * gelu_slope(u_s[slab, :, at : at + CHUNK])).astype(bf16)
            part = dot_last(du, w1[slab, :, at : at + CHUNK])
            total = part if total is None else total + part
    dh1 = (grad_two + total).astype(bf16)
    grad_one = normalise_back(dh1.astype(f32) * row(tail_ref, G1), normed_one, scale_one)
    token_ref[...] = grad_one
    dctx = dot_last(grad_one.astype(bf16), wo[...]).astype(bf16)
    attention_back(q_ref, k_ref, v_ref, dctx, item_masks(counts_ref, lengths_ref), dq_s, dk_s, dv_s)

    qkv.wait()
    dq, dk, dv = dq_s[...], dk_s[...], dv_s[...]
    daq = (2.0 * dot_last(dq, bq_ref[...])).astype(bf16)
    dav = (2.0 * dot_last(dv, bv_ref[...])).astype(bf16)
    aq = dot(x, a_ref[0]).astype(bf16)
    av = dot(x, a_ref[1]).astype(bf16)
    gq_ref[...] = 2.0 * dot_first(aq, dq)
    gv_ref[...] = 2.0 * dot_first(av, dv)
    token_ref[...] += (
        dot_last(dq, w[:WIDTH])
        + dot_last(dk, w[WIDTH : 2 * WIDTH])
        + dot_last(dv, w[2 * WIDTH :])
        + dot_last(daq, a_ref[0])
        + dot_last(dav, a_ref[1])
    )


def whole(shape):
    return pl.BlockSpec(shape, lambda *_: (0,) * len(shape))


ANY = pl.BlockSpec(memory_space=pl.ANY)
SCALARS = pl.BlockSpec(memory_space=pltpu.SMEM)
PARAMS = pltpu.CompilerParams(vmem_limit_bytes=VMEM)


def train_attention(counts, lengths, x, tail, a, bq, bv, w):
    rows = x.shape[0]
    shape = (rows, WIDTH)
    return pl.pallas_call(
        train_attention_kernel,
        in_specs=[SCALARS, SCALARS]
        + [whole(shape), whole(tail.shape), whole(a.shape), whole(bq.shape), whole(bv.shape), ANY],
        out_specs=[whole(shape)] * 4,
        out_shape=[jax.ShapeDtypeStruct(shape, bf16)] * 4,
        grid=(1,),
        scratch_shapes=[pltpu.VMEM((3, WIDTH, WIDTH), bf16), pltpu.SemaphoreType.DMA((3,))],
        compiler_params=PARAMS,
        name="train_attention",
    )(counts, lengths, x, tail, a, bq, bv, w)


def eval_attention(lengths, x, tail, a, bq, bv, w):
    rows = x.shape[0]
    block = pl.BlockSpec((BUCKET, WIDTH), lambda i: (i, 0))
    return pl.pallas_call(
        eval_attention_kernel,
        in_specs=[SCALARS, block]
        + [whole(tail.shape), whole(a.shape), whole(bq.shape), whole(bv.shape), ANY],
        out_specs=block,
        out_shape=jax.ShapeDtypeStruct((rows, WIDTH), bf16),
        grid=(rows // BUCKET,),
        scratch_shapes=[pltpu.VMEM((3, WIDTH, WIDTH), bf16)]
        + [pltpu.VMEM((BUCKET, WIDTH), bf16)] * 3
        + [pltpu.SemaphoreType.DMA((3,))],
        compiler_params=PARAMS,
        name="eval_attention",
    )(lengths, x, tail, a, bq, bv, w)


def eval_tail(x, ctx, tail, wo, w1, w2):
    rows = x.shape[0]
    block = pl.BlockSpec((BUCKET, WIDTH), lambda i: (i, 0))
    return pl.pallas_call(
        eval_tail_kernel,
        in_specs=[block, block, whole(tail.shape), ANY, ANY, ANY],
        out_specs=block,
        out_shape=jax.ShapeDtypeStruct((rows, WIDTH), bf16),
        grid=(rows // BUCKET,),
        scratch_shapes=[
            pltpu.VMEM((WIDTH, WIDTH), bf16),
            pltpu.VMEM((SLABS, WIDTH, WIDTH), bf16),
            pltpu.VMEM((SLABS, WIDTH, WIDTH), bf16),
            pltpu.SemaphoreType.DMA((1 + 2 * SLABS,)),
        ],
        compiler_params=PARAMS,
        name="eval_tail",
    )(x, ctx, tail, wo, w1, w2)


def train_rest(counts, lengths, x, q, k, v, ctx, grad, tail, a, bq, bv, w, wo, w1, w2):
    rows = x.shape[0]
    shape = (rows, WIDTH)
    return pl.pallas_call(
        train_kernel,
        in_specs=[SCALARS, SCALARS]
        + [whole(shape)] * 6
        + [whole(tail.shape), whole(a.shape), whole(bq.shape), whole(bv.shape)]
        + [ANY] * 4,
        out_specs=[whole(shape), whole(shape), whole(bq.shape), whole(bv.shape)],
        out_shape=[
            jax.ShapeDtypeStruct(shape, bf16),
            jax.ShapeDtypeStruct(shape, f32),
            jax.ShapeDtypeStruct(bq.shape, f32),
            jax.ShapeDtypeStruct(bv.shape, f32),
        ],
        grid=(1,),
        scratch_shapes=[
            pltpu.VMEM((QKV_ROWS, WIDTH), bf16),
            pltpu.VMEM((WIDTH, WIDTH), bf16),
            pltpu.VMEM((SLABS, WIDTH, WIDTH), bf16),
            pltpu.VMEM((SLABS, WIDTH, WIDTH), bf16),
            pltpu.VMEM((SLABS, rows, WIDTH), f32),
            pltpu.VMEM(shape, bf16),
            pltpu.VMEM(shape, bf16),
            pltpu.VMEM(shape, bf16),
            pltpu.SemaphoreType.DMA((2 + 2 * SLABS,)),
        ],
        compiler_params=PARAMS,
        name="train_rest",
    )(counts, lengths, x, q, k, v, ctx, grad, tail, a, bq, bv, w, wo, w1, w2)


def local(
    tokens,
    bucket_item_counts,
    slot_item_lengths,
    frozen,
    query_lowrank_matrix,
    value_lowrank_matrix,
    output_gradient,
    evaluation_tokens,
    evaluation_lengths,
    *,
    mesh,
):
    axes = ("fsdp", "rep")
    devices = mesh.shape["fsdp"] * mesh.shape["rep"]
    me = lax.axis_index(axes)
    share = WEIGHT_ROWS // devices
    extra = frozen.shape[0] - share * WIDTH
    spill = extra * devices
    before = lax.ppermute(
        frozen[-spill:], axes, [(d, (d + 1) % devices) for d in range(devices)]
    )
    window = lax.dynamic_slice(
        jnp.concatenate([before, frozen]), (spill - extra * me,), (share * WIDTH,)
    ).reshape(share, WIDTH)
    gathered = lax.all_gather(window, axes, axis=0, tiled=True)
    tail = lax.psum(jnp.where(me == devices - 1, frozen[-spill:].astype(f32), 0.0), axes).astype(bf16)
    vectors = tail[: VECTOR_ROWS * WIDTH].reshape(VECTOR_ROWS, WIDTH)
    vectors = jnp.pad(vectors, ((0, 16 - VECTOR_ROWS), (0, 0)))
    a = tail[VECTOR_ROWS * WIDTH :].reshape(2, WIDTH, RANK)
    bq = query_lowrank_matrix.astype(bf16)
    bv = value_lowrank_matrix.astype(bf16)
    wo = gathered[QKV_ROWS : QKV_ROWS + WIDTH]
    w1 = gathered[QKV_ROWS + WIDTH : QKV_ROWS + WIDTH * (1 + SLABS)]
    w1 = w1.reshape(WIDTH, SLABS, WIDTH).transpose(1, 0, 2)
    w2 = gathered[QKV_ROWS + WIDTH * (1 + SLABS) :].reshape(SLABS, WIDTH, WIDTH)

    ctx, q, k, v = train_attention(
        bucket_item_counts, slot_item_lengths, tokens, vectors, a, bq, bv, gathered
    )
    eval_ctx = eval_attention(evaluation_lengths, evaluation_tokens, vectors, a, bq, bv, gathered)
    out, token_gradient, gq, gv = train_rest(
        bucket_item_counts, slot_item_lengths, tokens, q, k, v, ctx, output_gradient,
        vectors, a, bq, bv, gathered, wo, w1, w2,
    )
    gq, gv = lax.psum((gq, gv), axes)
    eval_out = eval_tail(evaluation_tokens, eval_ctx, vectors, wo, w1, w2)
    return out, token_gradient, gq, gv, eval_out


def solution(mesh):
    split = P(("fsdp", "rep"), None)
    flat = P(("fsdp", "rep"))
    return jax.shard_map(
        functools.partial(local, mesh=mesh),
        mesh=mesh,
        in_specs=(split, split, split, flat, P(), P(), split, split, flat),
        out_specs=(split, split, P(), P(), split),
        check_vma=False,
    )
```

time: 694 us -> 314 us (0.45); the launches traced: 683 us -> 311 us
  matrix products: 259 us -> 0 us
  waiting for transfers between devices: 241 us -> 64 us
  Pallas kernels: 0 us -> 119 us
  local copies, waits for them, and re-layouts: 98.5 us -> 28.3 us
  blocking collectives: 40.5 us -> 79.9 us
  other arithmetic: 24 us -> 5.03 us
    unnamed x2 -> x1, waiting for transfers between devices: 241 us -> 0.02 us
    dot_general x35 -> x0, matrix products: 228 us -> none  [the longest x16 142 us: product_single_precision(): return jnp.dot(left, right, preferred_element_type=jnp.float32)]
    pallas_call x0 -> x4, Pallas kernels: none -> 119 us  [the longest x1 45.1 us: eval_tail(): pl.pallas_call(eval_tail_kernel, in_specs=[block, block, whole(tail.shape...]
    all_gather x0 -> x1, waiting for transfers between devices: none -> 56.3 us  [local(): gathered = lax.all_gather(window, axes, axis=0, tiled=True)]
    psum x1 -> x2, blocking collectives: 40.5 us -> 79.9 us  [the longest x1 40.4 us: local(): lax.psum(jnp.where(me == devices - 1, frozen[-spill:].astype(f32), 0.0),...]
    slice x12 -> x6, local copies, waits for them, and re-layouts: 44.3 us -> 11.2 us  [the longest x1 7.95 us: local(): w2 = gathered[QKV_ROWS + WIDTH * (1 + SLABS):].reshape(SLABS, WIDTH, WIDTH)]
    sub x4 -> x0, matrix products: 30.3 us -> none  [attend(): expo_scores = jnp.exp(scores - top_score)]
    unnamed x126 -> x0, local copies, waits for them, and re-layouts: 28.3 us -> none
  transfers between devices with their start and end apart: 1 -> 2, of which waited for: 1 -> 2; matrix products, arithmetic and copies ran while one was open for 1% -> 2% of each run, Pallas kernels for 0% -> 0%
where the time goes in v1:
time: 314 us; the launch traced here: 311 us
  Pallas kernels  119 us (38%)
  blocking collectives  79.9 us (25%)
  waiting for transfers between devices  64 us (20%)
  local copies, waits for them, and re-layouts  28.3 us (9%)
  between operations  14.3 us (5%)
  other arithmetic  5.03 us (2%)
    all_gather x1, waiting for transfers between devices, local(): gathered = lax.all_gather(window, axes, axis=0, tiled=True)  56.3 us
    pallas_call x1, Pallas kernels, eval_tail(): pl.pallas_call(eval_tail_kernel, in_specs=[block, block, whole(tail.shape...  45.1 us
    psum x1, blocking collectives, local(): lax.psum(jnp.where(me == devices - 1, frozen[-spill:].astype(f32), 0.0),...  40.4 us
    psum x1, blocking collectives, local(): gq, gv = lax.psum((gq, gv), axes)  39.6 us
    pallas_call x1, Pallas kernels, train_rest(): pl.pallas_call(train_kernel, in_specs=[SCALARS, SCALARS] + [whole(shape)]...  35.7 us
    pallas_call x1, Pallas kernels, eval_attention(): pl.pallas_call(eval_attention_kernel, in_specs=[SCALARS, block] + [whole(...  27.9 us
    reshape x2, local copies, waits for them, and re-layouts, local(): w1 = w1.reshape(WIDTH, SLABS, WIDTH).transpose(1, 0, 2)  14 us
    pallas_call x1, Pallas kernels, train_attention(): pl.pallas_call(train_attention_kernel, in_specs=[SCALARS, SCALARS] + [who...  10.2 us
  transfers between devices with their start and end apart: 2, of which 2 were waited for; matrix products, arithmetic and copies ran while one was open for 2% of the time, Pallas kernels for 0%

profile of v1, /device:TPU:0, one launch (start us, length us, event | category | flops | bytes accessed | tf_op | source)
XLA Modules:
  0.0 310.9 jit_solution(11022453071584712736)
XLA Ops:
  7.2 0.0 all-gather.2.cloned.1.call-start
  7.2 0.9 slice.29
  8.1 0.5 collective-permute-start
  8.6 7.6 %collective-permute-done = bf16[21504]{0:T(1024)(128)(2,1)S(1)} collective-permute-done((bf16[21504]{0:T(1024)(128)(2,1)S(1)}, bf16[21504]{0:T(1024)(128)(2,1)S(1)}, u32[]{:S(2)}, u32[]{:S(2)}) %collective-permute-start) | collective-permute-done | bytes 43040 | tf_op jit(solution)/shard_map/ppermute | solution.py:447
  16.2 1.5 fusion
  17.7 1.2 reshape.32
  18.9 0.0 all-gather.2.cloned.1.call-update
  18.9 0.9 convert_select_fusion
  19.8 40.4 %psum.21 = bf16[21504]{0:T(1024)(128)(2,1)S(1)} all-reduce(f32[21504]{0:T(1024)S(1)} %convert_select_fusion), channel_id=1, replica_groups=mesh['fsdp'=8,'rep'=4] {'fsdp','rep'}, use_global_device_ids=true, to_apply=%region_0.1 | all-reduce | flops 21504 | bytes 129024 | tf_op jit(solution)/shard_map/psum | solution.py:454
  60.2 1.2 reshape.31.a_ref
  61.5 1.3 convert_element_type.16.bq_ref
  62.8 1.3 convert_element_type.17.bv_ref
  64.1 0.6 pad.4.tail_ref
  64.8 56.3 %all-gather.2.cloned.1.call-done.w_any = bf16[9216,768]{1,0:T(8,128)(2,1)} async-done(((bf16[288,768]{1,0:T(8,128)(2,1)}), bf16[9216,768]{1,0:T(8,128)(2,1)}) %all-gather.2.cloned.1.call-update) | async-done | bytes 14155792 | tf_op jit(solution)/shard_map/all_gather | solution.py:453
  121.1 7.9 %fusion.1 = (bf16[3072,768]{1,0:T(8,128)(2,1)}, bf16[3072,768]{1,0:T(8,128)(2,1)}) fusion(bf16[9216,768]{1,0:T(8,128)(2,1)} %all-gather.2.cloned.1.call-done.w_any), kind=kLoop, calls=%fused_computation.5 | loop fusion | bytes 18874368 | tf_op jit(solution)/shard_map/slice | solution.py:463
  129.0 8.9 %reshape.33 = bf16[768,4,768]{2,1,0:T(4,128)(2,1)} reshape(bf16[3072,768]{1,0:T(8,128)(2,1)} %get-tuple-element.24) | data formatting | bytes 9437184 | tf_op jit(solution)/shard_map/reshape | solution.py:462
  137.9 5.1 %copy.16 = bf16[768,4,768]{2,0,1:T(8,128)(2,1)} copy(bf16[768,4,768]{2,1,0:T(4,128)(2,1)} %reshape.33) | data formatting | bytes 9437184 | tf_op jit(solution)/shard_map/reshape | solution.py:462
  143.0 2.4 slice.38.wo_any
  145.4 27.9 %eval_attention.1.ctx_ref = bf16[2048,768]{1,0:T(8,128)(2,1)} custom-call(s32[4]{0:T(128)} %lengths_ref.5, bf16[2048,768]{1,0:T(8,128)(2,1)} %x_ref.7, bf16[16,768]{1,0:T(8,128)(2,1)} %pad.4.tail_ref, bf16[2,768,8]{2,1,0:T(8,128)(2,1)} %reshape.31.a_ref, bf16[8,768]{1,0:T(8,128)(2,1)} %convert_element_type.16.bq_ref, ...), custom_call_target="tpu_custom_call" | custom-call | tf_op jit(solution)/shard_map/eval_attention/pallas_call | solution.py:360
  173.3 45.1 %eval_tail.1 = bf16[2048,768]{1,0:T(8,128)(2,1)} custom-call(bf16[2048,768]{1,0:T(8,128)(2,1)} %x_ref.7, bf16[2048,768]{1,0:T(8,128)(2,1)} %eval_attention.1.ctx_ref, bf16[16,768]{1,0:T(8,128)(2,1)} %pad.4.tail_ref, bf16[768,768]{1,0:T(8,128)(2,1)} %slice.38.wo_any, bf16[4,768,768]{2,1,0:T(8,128)(2,1)} %bitcast.4, bf16[4,768,768]{2,1,0:T(8,128)(2,1)} %bitcast.6), custom_call_target="tpu_custom_call" | custom-call | tf_op jit(solution)/shard_map/eval_tail/pallas_call | solution.py:378
  218.4 10.2 %train_attention.1 = (bf16[512,768]{1,0:T(8,128)(2,1)}, bf16[512,768]{1,0:T(8,128)(2,1)}, bf16[512,768]{1,0:T(8,128)(2,1)}, bf16[512,768]{1,0:T(8,128)(2,1)}) custom-call(s32[1,4]{1,0:T(1,128)} %counts_ref.3, s32[1,8]{1,0:T(1,128)} %lengths_ref.4, bf16[512,768]{1,0:T(8,128)(2,1)} %x_ref.5, bf16[16,768]{1,0:T(8,128)(2,1)} %pad.4.tail_ref, ...), custom_call_target="tpu_custom_call" | custom-call | tf_op jit(solution)/shard_map/train_attention/pallas_call | solution.py:344
  228.7 35.7 %train_rest.1 = (bf16[512,768]{1,0:T(8,128)(2,1)}, f32[512,768]{1,0:T(8,128)}, f32[8,768]{1,0:T(8,128)}, f32[8,768]{1,0:T(8,128)}) custom-call(s32[1,4]{1,0:T(1,128)} %counts_ref.3, s32[1,8]{1,0:T(1,128)} %lengths_ref.4, bf16[512,768]{1,0:T(8,128)(2,1)} %x_ref.5, bf16[512,768]{1,0:T(8,128)(2,1)} %get-tuple-element.13.q_ref, ...), custom_call_target="tpu_custom_call" | custom-call | tf_op jit(solution)/shard_map/train_rest/pallas_call | solution.py:398
  264.4 39.6 %all-reduce.1 = (f32[8,768]{1,0:T(8,128)}, f32[8,768]{1,0:T(8,128)}) all-reduce(f32[8,768]{1,0:T(8,128)} %get-tuple-element.19, f32[8,768]{1,0:T(8,128)} %get-tuple-element.20), channel_id=1, replica_groups=mesh['fsdp'=8,'rep'=4] {'fsdp','rep'}, use_global_device_ids=true, to_apply=%region_1.2 | all-reduce | flops 12288 | bytes 98304 | tf_op jit(solution)/shard_map/psum | solution.py:473
  (3 shorter events, 0.0 us)
Async XLA Ops:
  7.2 113.9 %all-gather.2.cloned.1.call-start = ((), (), s32[]{:S(2)}) async-start(), calls=%async_computation | async-start | bytes 14598144 | tf_op jit(solution)/shard_map/all_gather | solution.py:453
  8.1 8.1 %collective-permute-start = (bf16[21504]{0:T(1024)(128)(2,1)S(1)}, bf16[21504]{0:T(1024)(128)(2,1)S(1)}, u32[]{:S(2)}, u32[]{:S(2)}) collective-permute-start(bf16[21504]{0:T(1024)(128)(2,1)S(1)} %slice.29), channel_id=1, source_target_pairs={{0,1},{1,2},{2,3},{3,4},{4,5},{5,6},{6,7},{7,8},{8,9},{9,10},{10,1... | collective-permute-start | bytes 129032 | tf_op jit(solution)/shard_map/ppermute | solution.py:447
Sparse Core Ops, SparseCore 0:
  19.0 102.0 all-gather.1
